TPU v7x, 128 devices: a whole 4x4x4 slice. The times are simulated.
128 devices in a mesh: dp: 16 (over z, y_hi, core), mp: 8 (over x, y_lo).
Axes of the slice: x: 4, y: 4 (y_hi: 2, y_lo: 2; y = y_hi * 2 + y_lo), z: 4, core: 2. Of those that a mesh axis runs over, the one named last changes fastest.
Arguments:
- layer_inputs: bfloat16 [20480, 5120], P('dp', 'mp'), may hold values from -6 to 6
- cotangent: bfloat16 [20480, 7168], P('dp', 'mp'), may hold values from -0.41796875 to 0.41796875
- master: float32 [5120, 7168], P('dp', 'mp'), may hold values from -0.078125 to 0.078125
- moment_one: float32 [5120, 7168], P('dp', 'mp'), may hold values from -1.8 to 1.8
- moment_two: float32 [5120, 7168], P('dp', 'mp'), may hold values from 10 to 1000
- embedding_table: bfloat16 [76032, 5120], P('dp', 'mp'), may hold values from -6 to 6
- token_ids: int32 [256, 4], replicated, may hold values from 0 to 76031
- lengths: int32 [256], P('dp'), may hold values from 2 to 1024, as said below
- key_cache: bfloat16 [256, 8, 1024, 128], P('dp', 'mp'), may hold values from -2048 to 2048
- value_cache: bfloat16 [256, 8, 1024, 128], P('dp', 'mp'), may hold values from -6 to 6
Outputs:
- new_master: float32 [5120, 7168], P('dp', 'mp')
- new_moment_one: float32 [5120, 7168], P('dp', 'mp')
- new_moment_two: float32 [5120, 7168], P('dp', 'mp')
- attended: float32 [256, 4, 5120], P('dp', None, 'mp')
Inputs may be any that keep to these rules, and one draw needn't show every extreme that they name: lengths[s] slots of sequence s are filled; some sequence has all 1024.
All inputs are finite; a program needn't handle non-finite values.
Results may differ from a plain program's by a relative error of at most 0.022.
Values may be sent and summed in bfloat16 or wider, within the bound.
A program may use at most 128 MiB of HBM per device.

v0:
```python
import math

import jax
import jax.numpy as jnp
from jax import lax
from jax.sharding import PartitionSpec as P

QH = 40
KVH = 8


beta_one = 0.9
beta_two = 0.95
adam_eps = 1e-08
learn_rate = 0.001
decay_rate = 0.1
adam_step = 8
norm_eps = 1e-06
rope_base = 1000000.0


def rotate(vectors, positions):
    half_width = vectors.shape[-1] // 2
    frequency = jnp.exp(
        jnp.arange(half_width, dtype=jnp.float32) * (-2.0 * math.log(rope_base) / vectors.shape[-1])
    )
    angles = positions[:, :, None, None, None].astype(jnp.float32) * frequency
    cosine_table = jnp.cos(angles)
    sine_table = jnp.sin(angles)
    front_half = vectors[..., :half_width]
    back_half = vectors[..., half_width:]
    return jnp.concatenate(
        [
            front_half * cosine_table - back_half * sine_table,
            back_half * cosine_table + front_half * sine_table,
        ],
        axis=-1,
    )


def attend(joined, lengths, key_cache, value_cache, group_size):
    seq_count = joined.shape[0]
    step_count = joined.shape[1]
    kv_heads = key_cache.shape[1]
    cache_span = key_cache.shape[2]
    head_width = key_cache.shape[3]
    shaped = joined.reshape(seq_count, step_count, kv_heads, group_size + 2, head_width)
    positions = lengths[:, None] + jnp.arange(step_count, dtype=jnp.int32)[None, :]
    queries = rotate(shaped[:, :, :, :group_size], positions)
    new_keys = rotate(shaped[:, :, :, group_size : group_size + 1], positions)[:, :, :, 0].astype(
        jnp.bfloat16
    )
    new_values = shaped[:, :, :, group_size + 1].astype(jnp.bfloat16)
    score_scale = 1.0 / math.sqrt(head_width)
    old_scores = (
        jnp.einsum(
            "bskgd,bkcd->bskgc",
            queries,
            key_cache.astype(jnp.float32),
            precision=lax.Precision.HIGHEST,
        )
        * score_scale
    )
    new_scores = (
        jnp.einsum(
            "bskgd,btkd->bskgt",
            queries,
            new_keys.astype(jnp.float32),
            precision=lax.Precision.HIGHEST,
        )
        * score_scale
    )
    cache_live = jnp.arange(cache_span, dtype=jnp.int32)[None, :] < lengths[:, None]
    old_scores = jnp.where(cache_live[:, None, None, None, :], old_scores, -jnp.inf)
    causal = jnp.arange(step_count)[None, :] <= jnp.arange(step_count)[:, None]
    new_scores = jnp.where(causal[None, :, None, None, :], new_scores, -jnp.inf)
    row_max = jnp.maximum(jnp.max(old_scores, axis=-1), jnp.max(new_scores, axis=-1))[..., None]
    old_exp = jnp.exp(old_scores - row_max)
    new_exp = jnp.exp(new_scores - row_max)
    exp_total = jnp.sum(old_exp, axis=-1, keepdims=True) + jnp.sum(new_exp, axis=-1, keepdims=True)
    old_weights = (old_exp / exp_total).astype(jnp.bfloat16)
    new_weights = (new_exp / exp_total).astype(jnp.bfloat16)
    mixed_out = jnp.einsum(
        "bskgc,bkcd->bskgd", old_weights, value_cache, preferred_element_type=jnp.float32
    )
    mixed_out = mixed_out + jnp.einsum(
        "bskgt,btkd->bskgd", new_weights, new_values, preferred_element_type=jnp.float32
    )
    return mixed_out.reshape(seq_count, step_count, kv_heads * group_size * head_width)


def apply_adamw(master, moment_one, moment_two, gradient):
    first_new = beta_one * moment_one + (1.0 - beta_one) * gradient
    second_new = beta_two * moment_two + (1.0 - beta_two) * gradient * gradient
    first_hat = first_new / (1.0 - beta_one**adam_step)
    second_hat = second_new / (1.0 - beta_two**adam_step)
    updated = master - learn_rate * (
        first_hat / (jnp.sqrt(second_hat) + adam_eps) + decay_rate * master
    )
    return (updated, first_new, second_new)


def local(
    layer_inputs,
    cotangent,
    master,
    moment_one,
    moment_two,
    embedding_table,
    token_ids,
    lengths,
    key_cache,
    value_cache,
):
    full_inputs = lax.all_gather(layer_inputs, "mp", axis=1, tiled=True)
    gradient = lax.psum_scatter(
        lax.dot_general(
            full_inputs, cotangent, (((0,), (0,)), ((), ())), preferred_element_type=jnp.float32
        ).astype(jnp.bfloat16),
        "dp",
        scatter_dimension=0,
        tiled=True,
    ).astype(jnp.float32)
    new_master, new_moment_one, new_moment_two = apply_adamw(
        master, moment_one, moment_two, gradient
    )
    fresh = new_master.astype(jnp.bfloat16)
    vocab_rows = embedding_table.shape[0]
    offset = lax.axis_index("dp") * vocab_rows
    shifted = token_ids - offset
    inside = (shifted >= 0) & (shifted < vocab_rows)
    picked = jnp.take(embedding_table, jnp.clip(shifted, 0, vocab_rows - 1), axis=0)
    picked = jnp.where(inside[:, :, None], picked.astype(jnp.float32), 0.0)
    own_rows = lax.psum_scatter(picked.astype(jnp.bfloat16), "dp", scatter_dimension=0, tiled=True)
    embedded = lax.all_gather(own_rows, "mp", axis=2, tiled=True)
    widened = embedded.astype(jnp.float32)
    normed = (
        widened * lax.rsqrt(jnp.mean(widened * widened, axis=-1, keepdims=True) + norm_eps)
    ).astype(jnp.bfloat16)
    seq_count = normed.shape[0]
    step_count = normed.shape[1]
    model_width = normed.shape[2]
    flat_rows = normed.reshape(seq_count * step_count, model_width)
    joined = jnp.dot(
        flat_rows,
        lax.all_gather(fresh, "dp", axis=0, tiled=True),
        preferred_element_type=jnp.float32,
    )
    joined = joined.reshape(seq_count, step_count, fresh.shape[1])
    attended = attend(joined, lengths, key_cache, value_cache, QH // KVH)
    return (new_master, new_moment_one, new_moment_two, attended)


def solution(mesh):
    in_specs = (
        P("dp", "mp"),
        P("dp", "mp"),
        P("dp", "mp"),
        P("dp", "mp"),
        P("dp", "mp"),
        P("dp", "mp"),
        P(),
        P("dp"),
        P("dp", "mp", None, None),
        P("dp", "mp", None, None),
    )
    out_specs = (P("dp", "mp"), P("dp", "mp"), P("dp", "mp"), P("dp", None, "mp"))
    return jax.shard_map(local, mesh=mesh, in_specs=in_specs, out_specs=out_specs, check_vma=False)
```

profile of v0, /device:TPU:1, one launch (start us, length us, event | category | flops | bytes accessed | tf_op | source)
XLA Modules:
  0.0 584.2 jit_solution(16116390793163783579)
XLA Ops:
  7.2 0.0 copy-start
  7.2 0.0 all-gather.3.cloned.1.call-start
  7.2 0.7 all-gather.3.cloned.1.call-update
  7.9 0.0 reduce-scatter.3.cloned.1.call-start
  8.0 261.8 %all-gather.3.cloned.1.call-done = bf16[1280,5120]{1,0:T(8,128)(2,1)} async-done(((bf16[1280,640]{1,0:T(8,128)(2,1)}), bf16[1280,5120]{1,0:T(8,128)(2,1)}) %all-gather.3.cloned.1.call-update) | async-done | bytes 13107216 | tf_op jit(solution)/shard_map/all_gather | solution.py:115
  269.7 0.0 copy-done
  269.7 19.0 %convolution_convert_fusion = bf16[5120,896]{1,0:T(8,128)(2,1)} fusion(bf16[1280,5120]{1,0:T(8,128)(2,1)} %all-gather.3.cloned.1.call-done, bf16[1280,896]{1,0:T(8,128)(2,1)S(1)} %copy-done), kind=kOutput, calls=%fused_computation.1 | convolution fusion | flops 11748638720 | bytes 24576000 | tf_op jit(solution)/shard_map/dot_general | solution.py:117
  288.8 0.0 reduce-scatter.3.cloned.1.call-update
  288.8 0.0 reduce-scatter.5.cloned.1.call-start
  288.8 0.6 copy-done.6
  289.5 0.1 copy.20
  289.6 0.1 reshape.193
  289.7 7.7 %gather_fusion = bf16[1024,640]{1,0:T(8,128)(2,1)S(1)} fusion(bf16[4752,640]{1,0:T(8,128)(2,1)} %param.15, s32[1024]{0:T(1024)S(1)} %broadcast_clamp_fusion), kind=kCustom, calls=%fused_computation | custom fusion | bytes 2625536 | tf_op jit(solution)/shard_map/jit(_take)/gather | solution.py:132
  297.5 1.2 reshape.192
  298.7 2.7 select_convert_fusion
  301.4 0.0 reduce-scatter.5.cloned.1.call-update
  301.4 0.0 copy-start.7
  301.4 0.0 all-gather.5.cloned.1.call-start
  301.5 93.5 %reduce-scatter.3.cloned.1.call-done = bf16[320,896]{1,0:T(8,128)(2,1)} async-done(((bf16[5120,896]{1,0:T(8,128)(2,1)}), bf16[320,896]{1,0:T(8,128)(2,1)}) %reduce-scatter.3.cloned.1.call-update) | async-done | bytes 573456 | tf_op jit(solution)/shard_map/reduce_scatter | solution.py:116
  395.0 0.0 copy-done.4
  395.0 0.0 copy-done.5
  395.0 0.0 copy-done.3
  395.0 3.6 fusion.39
  398.6 0.0 all-gather.5.cloned.1.call-update
  398.7 0.0 copy-done.7
  398.7 0.1 iota_compare_fusion
  398.8 0.2 multiply_cosine_fusion.1
  399.0 66.1 %reduce-scatter.5.cloned.1.call-done = bf16[16,4,640]{2,0,1:T(8,128)(2,1)} async-done(((bf16[256,4,640]{2,0,1:T(8,128)(2,1)}), bf16[16,4,640]{2,0,1:T(8,128)(2,1)}) %reduce-scatter.5.cloned.1.call-update) | async-done | bytes 81936 | tf_op jit(solution)/shard_map/reduce_scatter | solution.py:134
  465.0 25.0 %all_gather.10 = bf16[16,4,5120]{2,0,1:T(8,128)(2,1)S(1)} all-gather(bf16[16,4,640]{2,0,1:T(8,128)(2,1)} %reduce-scatter.5.cloned.1.call-done), channel_id=1, replica_groups=mesh['dp'=16,'mp'=8] {'mp'}, dimensions={2}, use_global_device_ids=true | all-gather | bytes 737280 | tf_op jit(solution)/shard_map/all_gather | solution.py:135
  490.0 0.2 fusion.8
  490.2 59.4 %all-gather.5.cloned.1.call-done = bf16[5120,896]{1,0:T(8,128)(2,1)} async-done(((bf16[320,896]{1,0:T(8,128)(2,1)}), bf16[5120,896]{1,0:T(8,128)(2,1)}) %all-gather.5.cloned.1.call-update) | async-done | bytes 9175056 | tf_op jit(solution)/shard_map/all_gather | solution.py:146
  549.6 12.7 %copy.22 = bf16[896,5120]{1,0:T(8,128)(2,1)} copy(bf16[896,5120]{0,1:T(8,128)(2,1)} %bitcast.70) | data formatting | bytes 18350080 | tf_op jit(solution)/shard_map/dot_general | solution.py:144
  562.4 6.7 %convolution_bitcast_fusion = f32[16,4,1,7,128]{4,0,3,1,2:T(8,128)S(1)} fusion(bf16[7,128,5120,1]{2,1,0,3:T(8,128)(2,1)} %bitcast.71, bf16[16,4,5120]{2,0,1:T(8,128)(2,1)S(1)} %all_gather.10, f32[16,4]{0,1:T(4,128)S(1)} %add_rsqrt_fusion), kind=kOutput, calls=%fused_computation.22 | convolution fusion | flops 588185600 | bytes 10060032 | tf_op jit(solution)/shard_map/dot_general | solution.py:144
  569.0 0.2 fusion.33
  569.2 0.1 multiply_subtract_fusion.1
  569.4 0.1 maximum_bitcast_fusion
  569.5 0.1 maximum_bitcast_fusion.1
  569.6 0.0 copy-done.2
  569.6 3.5 fusion.42
  573.1 1.9 fusion.43
  575.0 0.5 fusion.5
  575.5 0.1 fusion.25
  575.6 0.0 copy-done.8
  575.7 0.0 copy-start.1
  575.7 1.0 fusion.10
  576.7 0.3 fusion.13
  576.9 0.7 reshape.207
  577.7 0.0 copy-done.1
  (15 shorter events, 0.1 us)
Async XLA Ops:
  7.2 262.6 %copy-start = (bf16[1280,896]{1,0:T(8,128)(2,1)S(1)}, bf16[1280,896]{1,0:T(8,128)(2,1)}, u32[]{:S(2)}) copy-start(bf16[1280,896]{1,0:T(8,128)(2,1)} %param.11) | copy-start | bytes 6881284
  7.2 262.5 %all-gather.3.cloned.1.call-start = ((), (), s32[]{:S(2)}) async-start(), calls=%async_computation.2 | async-start | bytes 14745600 | tf_op jit(solution)/shard_map/all_gather | solution.py:115
  7.9 387.1 %reduce-scatter.3.cloned.1.call-start = ((), (), s32[]{:S(2)}) async-start(), calls=%async_computation.3 | async-start | bytes 9748480 | tf_op jit(solution)/shard_map/reduce_scatter | solution.py:116
  288.8 0.7 copy-start.6
  288.8 176.2 %reduce-scatter.5.cloned.1.call-start = ((), (), s32[]{:S(2)}) async-start(), calls=%async_computation.4 | async-start | bytes 1392640 | tf_op jit(solution)/shard_map/reduce_scatter | solution.py:134
  298.7 96.3 %copy-start.4 = (f32[320,896]{1,0:T(8,128)S(1)}, f32[320,896]{1,0:T(8,128)}, u32[]{:S(2)}) copy-start(f32[320,896]{1,0:T(8,128)} %param.13) | copy-start | bytes 3440644
  298.7 96.3 %copy-start.5 = (f32[320,896]{1,0:T(8,128)S(1)}, f32[320,896]{1,0:T(8,128)}, u32[]{:S(2)}) copy-start(f32[320,896]{1,0:T(8,128)} %param.14) | copy-start | bytes 3440644
  301.4 93.6 %copy-start.3 = (f32[320,896]{1,0:T(8,128)S(1)}, f32[320,896]{1,0:T(8,128)}, u32[]{:S(2)}) copy-start(f32[320,896]{1,0:T(8,128)} %param.12) | copy-start | bytes 3440644
  301.4 97.3 %copy-start.7 = (s32[16]{0:T(128)S(1)}, s32[16]{0:T(128)}, u32[]{:S(2)}) copy-start(s32[16]{0:T(128)} %param.17) | copy-start | bytes 196
  301.4 248.2 %all-gather.5.cloned.1.call-start = ((), (), s32[]{:S(2)}) async-start(), calls=%async_computation.5 | async-start | bytes 9748480 | tf_op jit(solution)/shard_map/all_gather | solution.py:146
  562.4 7.2 %copy-start.2 = (bf16[16,1,1024,128]{3,2,1,0:T(8,128)(2,1)S(1)}, bf16[16,1,1024,128]{3,2,1,0:T(8,128)(2,1)}, u32[]{:S(2)}) copy-start(bf16[16,1,1024,128]{3,2,1,0:T(8,128)(2,1)} %param.18) | copy-start | bytes 12582916
  569.6 6.1 %copy-start.8 = (bf16[16,1,1024,128]{3,2,1,0:T(8,128)(2,1)S(1)}, bf16[16,1,1024,128]{3,2,1,0:T(8,128)(2,1)}, u32[]{:S(2)}) copy-start(bf16[16,1,1024,128]{3,2,1,0:T(8,128)(2,1)} %param.19) | copy-start | bytes 12582916
  575.7 2.0 copy-start.1
Sparse Core Ops, SparseCore 0:
  9.7 260.0 all-gather.2
  288.9 106.0 reduce-scatter.2
  398.9 66.0 reduce-scatter.4
  467.7 81.8 all-gather.4
where the time goes:
time: 585 us; the launch traced here: 584 us
  waiting for transfers between devices  481 us (82%)
  matrix products  32.3 us (6%)
  blocking collectives  25 us (4%)
  local copies, waits for them, and re-layouts  23.3 us (4%)
  between operations  13.9 us (2%)
  other arithmetic  7.99 us (1%)
    all_gather x1, waiting for transfers between devices, local(): full_inputs = lax.all_gather(layer_inputs, 'mp', axis=1, tiled=True)  262 us
    reduce_scatter x1, waiting for transfers between devices, local(): lax.psum_scatter(lax.dot_general(full_inputs, cotangent, (((0,), (0,)), (...  93.5 us
    reduce_scatter x1, waiting for transfers between devices, local(): lax.psum_scatter(picked.astype(jnp.bfloat16), 'dp', scatter_dimension=0,...  66.1 us
    all_gather x1, waiting for transfers between devices, local(): lax.all_gather(fresh, 'dp', axis=0, tiled=True)  59.4 us
    all_gather x1, blocking collectives, local(): embedded = lax.all_gather(own_rows, 'mp', axis=2, tiled=True)  25 us
    dot_general x1, matrix products, local(): lax.dot_general(full_inputs, cotangent, (((0,), (0,)), ((), ())), preferr...  19 us
    dot_general x1, local copies, waits for them, and re-layouts, local(): jnp.dot(flat_rows, lax.all_gather(fresh, 'dp', axis=0, tiled=True), prefe...  12.7 us
  transfers between devices with their start and end apart: 4, of which 4 were waited for; matrix products, arithmetic and copies ran while one was open for 3% of the time, Pallas kernels for 0%

commit v1 on v0

--- a/solution.py
+++ b/solution.py
@@ -3,6 +3,8 @@
 import jax
 import jax.numpy as jnp
 from jax import lax
+from jax.experimental import pallas as pl
+from jax.experimental.pallas import tpu as pltpu
 from jax.sharding import PartitionSpec as P
 
 QH = 40
@@ -100,6 +102,287 @@
     return (updated, first_new, second_new)
 
 
+MESH = pl.DeviceIdType.MESH
+CHUNKS = ((0, 0, 896), (1, 0, 512), (1, 512, 384))
+ROUNDS = 5
+R = 64
+
+
+def place():
+    d = lax.axis_index("dp")
+    m = lax.axis_index("mp")
+    return d // 4, (d // 2) % 2, d % 2, m // 2, m % 2
+
+
+def at(z, h, c, x, l):
+    return {"dp": z * 4 + h * 2 + c, "mp": x * 2 + l}
+
+
+def remote(src, dst, send_sem, recv_sem, device):
+    return pltpu.make_async_remote_copy(
+        src_ref=src, dst_ref=dst, send_sem=send_sem, recv_sem=recv_sem,
+        device_id=device, device_id_type=MESH,
+    )
+
+
+def gradient_kernel(
+    x_ref, c_ref, g_ref,
+    xt, xg, cg, sums0, sums1, sums2, part0, part1, part2,
+    half_l0, half_l1, half_l2, half_r0, half_r1, half_r2,
+    full_l0, full_l1, full_l2, full_r0, full_r1, full_r2,
+    ysend0, ysend1, ysend2, one0, one1, one2, two1, two2,
+    local_sem, swap_s, swap_r, own_s, own_r, fwd_s, fwd_r, csib_s, csib_r, cy_s, cy_r, cf_s, cf_r,
+    hs, hr, fs, fr, ys, yr,
+):
+    z, h, c, x, l = place()
+    sib = at(z, h, 1 - c, x, l)
+    xr = at(z, h, c, (x + 1) % 4, l)
+    xl = at(z, h, c, (x + 3) % 4, l)
+    zr = at((z + 1) % 4, h, c, x, l)
+    zl = at((z + 3) % 4, h, c, x, l)
+    y_l = at(z, h, c, x, 1 - l)
+    y_h = at(z, 1 - h, c, x, l)
+    y_b = at(z, 1 - h, c, x, 1 - l)
+    home = h == l
+    sums = (sums0, sums1, sums2)
+    part = (part0, part1, part2)
+    half_l = (half_l0, half_l1, half_l2)
+    half_r = (half_r0, half_r1, half_r2)
+    full_l = (full_l0, full_l1, full_l2)
+    full_r = (full_r0, full_r1, full_r2)
+    ysend = (ysend0, ysend1, ysend2)
+    one = (one0, one1, one2)
+    two = (None, two1, two2)
+
+    c_local = pltpu.make_async_copy(c_ref, cg.at[0, pl.ds(0, 1280)], local_sem)
+    c_local.start()
+    peers = (sib, xr, xl, zr, zl, y_l, y_h, y_b)
+    barrier = pltpu.get_barrier_semaphore()
+    for peer in peers:
+        pl.semaphore_signal(barrier, inc=1, device_id=peer, device_id_type=MESH)
+    pl.semaphore_wait(barrier, len(peers))
+
+    started = []
+
+    def go(copy):
+        copy.start()
+        started.append(copy)
+
+    def c_cols(j):
+        _, lo, width = CHUNKS[j]
+        return pl.ds(lo, width)
+
+    for j in (1, 2):
+        go(remote(c_ref.at[:, c_cols(j)], cg.at[1, pl.ds(0, 1280), c_cols(j)], cy_s.at[j - 1], cy_r.at[j - 1], y_l))
+
+    def transpose(j):
+        block = x_ref[:, 128 * j : 128 * j + 128].T
+        for s in range(2):
+            feature = 128 * j + 64 * s
+            xt[feature // 320, feature % 320 : feature % 320 + 64, :] = block[64 * s : 64 * s + 64]
+
+    def rows(k):
+        return pl.ds(R * k, R)
+
+    def swap(k):
+        go(remote(xt.at[1 - c, rows(k)], xg.at[x, rows(k), pl.ds(1280, 1280)], swap_s.at[k], swap_r.at[k], sib))
+        xg[x, R * k : R * k + R, 0:1280] = xt[c, R * k : R * k + R, :]
+
+    transpose(0)
+    transpose(2)
+    swap(0)
+    go(remote(c_ref, cg.at[0, pl.ds(1280, 1280)], csib_s, csib_r, sib))
+    transpose(3)
+    swap(1)
+    transpose(1)
+    swap(2)
+    transpose(4)
+    swap(3)
+    swap(4)
+
+    x_left, x_right, x_far = (x + 3) % 4, (x + 1) % 4, (x + 2) % 4
+
+    def send_own(k):
+        landed = xg.at[x, rows(k), pl.ds(1280, 1280)]
+        remote(landed, landed, swap_s.at[k], swap_r.at[k], sib).wait_recv()
+        block = xg.at[x, rows(k)]
+        go(remote(block, block, own_s.at[0, k], own_r.at[0, k], xr))
+        go(remote(block, block, own_s.at[1, k], own_r.at[1, k], xl))
+
+    def far_rows(k, side):
+        return pl.ds(R * k + side * (R // 2), R // 2)
+
+    def forward(k):
+        block = xg.at[x_left, rows(k)]
+        remote(block, block, own_s.at[0, k], own_r.at[0, k], xr).wait_recv()
+        block = xg.at[x_left, far_rows(k, 0)]
+        go(remote(block, block, fwd_s.at[0, k], fwd_r.at[0, k], xr))
+        block = xg.at[x_right, rows(k)]
+        remote(block, block, own_s.at[1, k], own_r.at[1, k], xl).wait_recv()
+        block = xg.at[x_right, far_rows(k, 1)]
+        go(remote(block, block, fwd_s.at[1, k], fwd_r.at[1, k], xl))
+
+    def wait_far(k):
+        for side, device in ((0, xr), (1, xl)):
+            block = xg.at[x_far, far_rows(k, side)]
+            remote(block, block, fwd_s.at[side, k], fwd_r.at[side, k], device).wait_recv()
+
+    def c_forward(j):
+        block = cg.at[1, pl.ds(0, 1280), c_cols(j)]
+        remote(block, block, cy_s.at[j - 1], cy_r.at[j - 1], y_l).wait_recv()
+        go(remote(block, cg.at[1, pl.ds(1280, 1280), c_cols(j)], cf_s.at[j - 1], cf_r.at[j - 1], sib))
+
+    def c_wait(j):
+        block = cg.at[1, pl.ds(1280, 1280), c_cols(j)]
+        remote(block, block, cf_s.at[j - 1], cf_r.at[j - 1], sib).wait_recv()
+
+    low, high = slice(0, R // 2), slice(R // 2, R)
+    dlow, dhigh = pl.ds(0, R // 2), pl.ds(R // 2, R // 2)
+
+    def multiply(k, j):
+        half, lo, width = CHUNKS[j]
+        lhs = jnp.concatenate([xg[(z + r) % 4, R * k : R * k + R, :] for r in range(4)], axis=0)
+        product = jnp.dot(lhs, cg[half, :, lo : lo + width], preferred_element_type=jnp.float32)
+        sums[j][k] = product[0:R]
+        for r in (1, 2, 3):
+            part[j][r - 1, k] = product[R * r : R * r + R].astype(jnp.bfloat16)
+        go(remote(part[j].at[1, k, dlow], half_l[j].at[k], hs.at[0, j, k], hr.at[0, j, k], zr))
+        go(remote(part[j].at[1, k, dhigh], half_r[j].at[k], hs.at[1, j, k], hr.at[1, j, k], zl))
+
+    def combine(k, j):
+        remote(half_l[j].at[k], half_l[j].at[k], hs.at[0, j, k], hr.at[0, j, k], zr).wait_recv()
+        part[j][0, k, low] = (part[j][0, k, low].astype(jnp.float32) + half_l[j][k].astype(jnp.float32)).astype(jnp.bfloat16)
+        go(remote(part[j].at[0, k], full_l[j].at[k], fs.at[0, j, k], fr.at[0, j, k], zr))
+        remote(half_r[j].at[k], half_r[j].at[k], hs.at[1, j, k], hr.at[1, j, k], zl).wait_recv()
+        part[j][2, k, high] = (part[j][2, k, high].astype(jnp.float32) + half_r[j][k].astype(jnp.float32)).astype(jnp.bfloat16)
+        go(remote(part[j].at[2, k], full_r[j].at[k], fs.at[1, j, k], fr.at[1, j, k], zl))
+
+    def y_copies(k, j):
+        src = ysend[j].at[k]
+        if j == 0:
+            return None, remote(src, one[j].at[k], ys.at[j, k], yr.at[0, j, k], y_h)
+        return (
+            remote(src, one[j].at[k], ys.at[j, k], yr.at[0, j, k], y_l),
+            remote(src, two[j].at[k], ys.at[j, k], yr.at[1, j, k], y_b),
+        )
+
+    def total(k, j):
+        remote(full_l[j].at[k], full_l[j].at[k], fs.at[0, j, k], fr.at[0, j, k], zr).wait_recv()
+        remote(full_r[j].at[k], full_r[j].at[k], fs.at[1, j, k], fr.at[1, j, k], zl).wait_recv()
+        value = sums[j][k] + full_l[j][k].astype(jnp.float32) + full_r[j][k].astype(jnp.float32)
+        at_home, away = y_copies(k, j)
+        if j == 0:
+            sums[j][k] = value
+        ysend[j][k] = value.astype(jnp.bfloat16)
+        if at_home is not None:
+            pl.when(home)(at_home.start)
+        pl.when(jnp.logical_not(home))(away.start)
+
+    def finish(k, j):
+        at_home, away = y_copies(k, j)
+        _, lo, width = CHUNKS[j]
+        if j == 0:
+            @pl.when(home)
+            def _():
+                away.wait_recv()
+                g_ref[R * k : R * k + R, :] = sums[j][k] + one[j][k].astype(jnp.float32)
+        else:
+            @pl.when(jnp.logical_not(home))
+            def _():
+                at_home.wait_recv()
+                away.wait_recv()
+                g_ref[R * k : R * k + R, lo : lo + width] = one[j][k].astype(jnp.float32) + two[j][k].astype(jnp.float32)
+
+    order = []
+
+    def step(tile):
+        order.append(tile)
+        n = len(order)
+        if tile is not None:
+            multiply(*tile)
+        for lag, stage in ((1, combine), (2, total), (3, finish)):
+            if n > lag and order[n - 1 - lag] is not None:
+                stage(*order[n - 1 - lag])
+
+    send_own(0)
+    send_own(1)
+    landed = cg.at[0, pl.ds(1280, 1280)]
+    forward(0)
+    send_own(2)
+    c_local.wait()
+    remote(landed, landed, csib_s, csib_r, sib).wait_recv()
+    forward(1)
+    send_own(3)
+    wait_far(0)
+    step((0, 0))
+    forward(2)
+    send_own(4)
+    wait_far(1)
+    step((1, 0))
+    c_forward(1)
+    forward(3)
+    wait_far(2)
+    step((2, 0))
+    c_wait(1)
+    step((0, 1))
+    step((1, 1))
+    step((2, 1))
+    forward(4)
+    wait_far(3)
+    step((3, 0))
+    step((3, 1))
+    c_forward(2)
+    wait_far(4)
+    step((4, 0))
+    step((4, 1))
+    c_wait(2)
+    for k in range(5):
+        step((k, 2))
+    for _ in range(3):
+        step(None)
+
+    for copy in started:
+        copy.wait_send()
+    for j in range(3):
+        for k in range(5):
+            at_home, away = y_copies(k, j)
+            if at_home is not None:
+                pl.when(home)(at_home.wait_send)
+            pl.when(jnp.logical_not(home))(away.wait_send)
+
+
+def gradient_of(layer_inputs, cotangent):
+    bf, f32 = jnp.bfloat16, jnp.float32
+    widths = [width for _, _, width in CHUNKS]
+    dma = pltpu.SemaphoreType.DMA
+    vm = pltpu.VMEM
+    scratch = [vm((2, 320, 1280), bf), vm((4, 320, 2560), bf), vm((2, 2560, 896), bf)]
+    scratch += [vm((5, R, w), f32) for w in widths]
+    scratch += [vm((3, 5, R, w), bf) for w in widths]
+    scratch += [vm((5, R // 2, w), bf) for w in widths] * 2
+    scratch += [vm((5, R, w), bf) for w in widths] * 2
+    scratch += [vm((5, R, w), bf) for w in widths]
+    scratch += [vm((5, R, w), bf) for w in widths]
+    scratch += [vm((5, R, w), bf) for w in widths[1:]]
+    scratch += [
+        dma(()), dma((5,)), dma((5,)), dma((2, 5)), dma((2, 5)), dma((2, 5)), dma((2, 5)),
+        dma(()), dma(()), dma((2,)), dma((2,)), dma((2,)), dma((2,)),
+        dma((2, 3, 5)), dma((2, 3, 5)), dma((2, 3, 5)), dma((2, 3, 5)), dma((3, 5)), dma((2, 3, 5)),
+    ]
+    return pl.pallas_call(
+        gradient_kernel,
+        out_shape=jax.ShapeDtypeStruct((320, 896), f32),
+        in_specs=[pl.BlockSpec(memory_space=pltpu.VMEM), pl.BlockSpec(memory_space=pl.ANY)],
+        out_specs=pl.BlockSpec(memory_space=pltpu.VMEM),
+        scratch_shapes=scratch,
+        compiler_params=pltpu.CompilerParams(
+            collective_id=1, has_side_effects=True, vmem_limit_bytes=60 * 1024 * 1024
+        ),
+        cost_estimate=pl.CostEstimate(flops=11_700_000_000, bytes_accessed=5_000_000, transcendentals=0),
+        name="gradient",
+    )(layer_inputs, cotangent)
+
+
 def local(
     layer_inputs,
     cotangent,
@@ -112,15 +395,7 @@
     key_cache,
     value_cache,
 ):
-    full_inputs = lax.all_gather(layer_inputs, "mp", axis=1, tiled=True)
-    gradient = lax.psum_scatter(
-        lax.dot_general(
-            full_inputs, cotangent, (((0,), (0,)), ((), ())), preferred_element_type=jnp.float32
-        ).astype(jnp.bfloat16),
-        "dp",
-        scatter_dimension=0,
-        tiled=True,
-    ).astype(jnp.float32)
+    gradient = gradient_of(layer_inputs, cotangent)
     new_master, new_moment_one, new_moment_two = apply_adamw(
         master, moment_one, moment_two, gradient
     )

time: 585 us -> 250 us (0.43)
  waiting for transfers between devices: 481 us -> 62.6 us
  Pallas kernels: 0 us -> 105 us
  matrix products: 32.3 us -> 13.3 us
    all_gather x1 -> x0, waiting for transfers between devices: 262 us -> none  [local(): full_inputs = lax.all_gather(layer_inputs, 'mp', axis=1, tiled=True)]
    pallas_call x0 -> x1, Pallas kernels: none -> 105 us  [gradient_of(): pl.pallas_call(gradient_kernel, out_shape=jax.ShapeDtypeStruct((320, 896)...]
    reduce_scatter x1 -> x0, waiting for transfers between devices: 93.5 us -> none  [local(): lax.psum_scatter(lax.dot_general(full_inputs, cotangent, (((0,), (0,)), (...]
    reduce_scatter x1, waiting for transfers between devices: 66.1 us -> 0.02 us  [local(): lax.psum_scatter(picked.astype(jnp.bfloat16), 'dp', scatter_dimension=0,...]
    dot_general x1 -> x0, matrix products: 19 us -> none  [local(): lax.dot_general(full_inputs, cotangent, (((0,), (0,)), ((), ())), preferr...]
  transfers between devices with their start and end apart: 4 -> 2, of which waited for: 4 -> 1; matrix products, arithmetic and copies ran while one was open for 3% -> 2% of each run, Pallas kernels for 0% -> 42%
where the time goes in v1:
time: 250 us; the launch traced here: 249 us
  Pallas kernels  105 us (42%)
  waiting for transfers between devices  62.6 us (25%)
  blocking collectives  24.8 us (10%)
  local copies, waits for them, and re-layouts  21.8 us (9%)
  between operations  14.3 us (6%)
  matrix products  13.3 us (5%)
  other arithmetic  7.54 us (3%)
    pallas_call x1, Pallas kernels, gradient_of(): pl.pallas_call(gradient_kernel, out_shape=jax.ShapeDtypeStruct((320, 896)...  105 us
    all_gather x1, waiting for transfers between devices, local(): lax.all_gather(fresh, 'dp', axis=0, tiled=True)  62.6 us
    all_gather x1, blocking collectives, local(): embedded = lax.all_gather(own_rows, 'mp', axis=2, tiled=True)  24.8 us
    dot_general x1, local copies, waits for them, and re-layouts, local(): jnp.dot(flat_rows, lax.all_gather(fresh, 'dp', axis=0, tiled=True), prefe...  12.7 us
    gather x2, local copies, waits for them, and re-layouts, local(): jnp.take(embedding_table, jnp.clip(shifted, 0, vocab_rows - 1), axis=0)  8.04 us
    dot_general x1, matrix products, local(): jnp.dot(flat_rows, lax.all_gather(fresh, 'dp', axis=0, tiled=True), prefe...  6.66 us
  transfers between devices with their start and end apart: 2, of which 1 were waited for; matrix products, arithmetic and copies ran while one was open for 2% of the time, Pallas kernels for 42%

profile of v1, /device:TPU:1, one launch (start us, length us, event | category | flops | bytes accessed | tf_op | source)
XLA Modules:
  0.0 249.0 jit_solution(8176983337746891522)
XLA Ops:
  7.2 0.0 reduce-scatter.2.cloned.1.call-start
  7.2 0.7 compare_and_fusion
  7.9 0.1 copy.20
  8.1 0.1 reshape.193
  8.2 7.7 %gather_fusion = bf16[1024,640]{1,0:T(8,128)(2,1)S(1)} fusion(bf16[4752,640]{1,0:T(8,128)(2,1)} %param.15, s32[1024]{0:T(1024)S(1)} %broadcast_clamp_fusion), kind=kCustom, calls=%fused_computation | custom fusion | bytes 2625536 | tf_op jit(solution)/shard_map/jit(_take)/gather | solution.py:407
  15.9 0.3 reshape.192
  16.2 1.4 select_convert_fusion
  17.6 0.0 reduce-scatter.2.cloned.1.call-update
  17.7 0.0 copy-start.1
  17.7 0.0 copy-start.2
  17.7 0.0 copy-start.3
  17.7 0.0 all-gather.2.cloned.1.call-start
  17.7 104.7 %gradient.1 = f32[320,896]{1,0:T(8,128)} custom-call(bf16[1280,640]{1,0:T(8,128)(2,1)} %x_ref.1, bf16[1280,896]{1,0:T(8,128)(2,1)} %c_ref.1), custom_call_target="tpu_custom_call" | custom-call | flops 11699999744 | bytes 5000000 | tf_op jit(solution)/shard_map/gradient/pallas_call | solution.py:372
  122.4 0.0 copy-done.1
  122.4 0.0 copy-done.2
  122.4 0.0 copy-done.3
  122.4 0.0 copy-start.4
  122.5 3.8 %fusion.38 = (bf16[320,896]{1,0:T(8,128)(2,1)}, f32[320,896]{1,0:T(8,128)}, f32[320,896]{1,0:T(8,128)}, f32[320,896]{1,0:T(8,128)}) fusion(f32[320,896]{1,0:T(8,128)S(1)} %copy-done.1, f32[320,896]{1,0:T(8,128)} %gradient.1, f32[320,896]{1,0:T(8,128)S(1)} %copy-done.2, f32[320,896]{1,0:T(8,128)S(1)} %copy-done.3), kind=kLoop, calls=%fused_computation.67 | loop fusion | flops 4587520 | bytes 8601600 | tf_op jit(solution)/shard_map/convert_element_type | solution.py:402
  126.2 0.0 all-gather.2.cloned.1.call-update
  126.3 0.0 copy-done.4
  126.3 0.1 iota_compare_fusion
  126.4 0.2 multiply_cosine_fusion.1
  126.6 0.0 reduce-scatter.2.cloned.1.call-done
  126.6 24.8 %all_gather.6 = bf16[16,4,5120]{2,0,1:T(8,128)(2,1)S(1)} all-gather(bf16[16,4,640]{2,0,1:T(8,128)(2,1)} %reduce-scatter.2.cloned.1.call-done), channel_id=1, replica_groups=mesh['dp'=16,'mp'=8] {'mp'}, dimensions={2}, use_global_device_ids=true | all-gather | bytes 737280 | tf_op jit(solution)/shard_map/all_gather | solution.py:410
  151.4 0.2 fusion.8
  151.6 62.6 %all-gather.2.cloned.1.call-done = bf16[5120,896]{1,0:T(8,128)(2,1)} async-done(((bf16[320,896]{1,0:T(8,128)(2,1)}), bf16[5120,896]{1,0:T(8,128)(2,1)}) %all-gather.2.cloned.1.call-update) | async-done | bytes 9175056 | tf_op jit(solution)/shard_map/all_gather | solution.py:421
  214.2 12.7 %copy.22 = bf16[896,5120]{1,0:T(8,128)(2,1)} copy(bf16[896,5120]{0,1:T(8,128)(2,1)} %bitcast.68) | data formatting | bytes 18350080 | tf_op jit(solution)/shard_map/dot_general | solution.py:419
  226.9 0.0 copy-start
  226.9 6.7 %convolution_bitcast_fusion = f32[16,4,1,7,128]{4,0,3,1,2:T(8,128)S(1)} fusion(bf16[7,128,5120,1]{2,1,0,3:T(8,128)(2,1)} %bitcast.69, bf16[16,4,5120]{2,0,1:T(8,128)(2,1)S(1)} %all_gather.6, f32[16,4]{0,1:T(4,128)S(1)} %add_rsqrt_fusion), kind=kOutput, calls=%fused_computation.20 | convolution fusion | flops 588185600 | bytes 10060032 | tf_op jit(solution)/shard_map/dot_general | solution.py:419
  233.5 0.2 fusion.32
  233.8 0.1 multiply_subtract_fusion.1
  233.9 0.1 maximum_bitcast_fusion
  234.0 0.1 maximum_bitcast_fusion.1
  234.1 0.0 copy-done
  234.1 0.0 copy-start.5
  234.1 3.5 %fusion.40 = (f32[16,4,5]{2,1,0:T(4,128)S(1)}, f32[16,4,1,5,1024]{4,3,1,0,2:T(8,128)S(1)}) fusion(bf16[16,1,1024,128]{3,2,1,0:T(8,128)(2,1)S(1)} %copy-done, f32[16,4,5,128]{3,0,2,1:T(8,128)S(1)} %maximum_bitcast_fusion, pred[16,1024]{1,0:T(8,128)(4,1)S(1)} %iota_compare_fusion), kind=kOutput, calls=%fused_computation.68 | convolution fusion | flops 504299200 | bytes 5686528 | tf_op jit(solution)/shard_map/bskgd,bkcd->bskgc/dot_general | solution.py:58
  237.6 1.9 fusion.41
  239.5 0.5 fusion.5
  240.0 0.1 fusion.24
  240.2 0.0 copy-done.5
  240.2 1.0 fusion.10
  241.2 0.3 fusion.13
  241.4 0.7 reshape.207
  (8 shorter events, 0.1 us)
Async XLA Ops:
  7.2 119.4 %reduce-scatter.2.cloned.1.call-start = ((), (), s32[]{:S(2)}) async-start(), calls=%async_computation.1 | async-start | bytes 1392640 | tf_op jit(solution)/shard_map/reduce_scatter | solution.py:409
  17.7 104.8 %copy-start.1 = (f32[320,896]{1,0:T(8,128)S(1)}, f32[320,896]{1,0:T(8,128)}, u32[]{:S(2)}) copy-start(f32[320,896]{1,0:T(8,128)} %param.12) | copy-start | bytes 3440644
  17.7 104.8 %copy-start.2 = (f32[320,896]{1,0:T(8,128)S(1)}, f32[320,896]{1,0:T(8,128)}, u32[]{:S(2)}) copy-start(f32[320,896]{1,0:T(8,128)} %param.13) | copy-start | bytes 3440644
  17.7 104.8 %copy-start.3 = (f32[320,896]{1,0:T(8,128)S(1)}, f32[320,896]{1,0:T(8,128)}, u32[]{:S(2)}) copy-start(f32[320,896]{1,0:T(8,128)} %param.14) | copy-start | bytes 3440644
  17.7 196.5 %all-gather.2.cloned.1.call-start = ((), (), s32[]{:S(2)}) async-start(), calls=%async_computation.2 | async-start | bytes 9748480 | tf_op jit(solution)/shard_map/all_gather | solution.py:421
  122.4 3.8 %copy-start.4 = (s32[16]{0:T(128)S(1)}, s32[16]{0:T(128)}, u32[]{:S(2)}) copy-start(s32[16]{0:T(128)} %param.17) | copy-start | bytes 196
  226.9 7.2 %copy-start = (bf16[16,1,1024,128]{3,2,1,0:T(8,128)(2,1)S(1)}, bf16[16,1,1024,128]{3,2,1,0:T(8,128)(2,1)}, u32[]{:S(2)}) copy-start(bf16[16,1,1024,128]{3,2,1,0:T(8,128)(2,1)} %param.18) | copy-start | bytes 12582916
  234.1 6.1 %copy-start.5 = (bf16[16,1,1024,128]{3,2,1,0:T(8,128)(2,1)S(1)}, bf16[16,1,1024,128]{3,2,1,0:T(8,128)(2,1)}, u32[]{:S(2)}) copy-start(bf16[16,1,1024,128]{3,2,1,0:T(8,128)(2,1)} %param.19) | copy-start | bytes 12582916
Sparse Core Ops, SparseCore 0:
  17.8 73.9 reduce-scatter.1
  126.4 87.7 all-gather.1
